TPU v7x, 512 devices: a whole 4x4x16 slice. The times are simulated.
512 devices in a mesh: phase: 4 (over x), expert: 32 (over z_hi, y, core), tensor: 4 (over z_lo).
Axes of the slice: x: 4, y: 4, z: 16 (z_hi: 4, z_lo: 4; z = z_hi * 4 + z_lo), core: 2. Of those that a mesh axis runs over, the one named last changes fastest.
Arguments:
- forward_routes: int32 [4, 2048, 6], P('phase', 'expert'), may hold values from 0 to 95, all different within a row; in each aligned block of 64 rows (0 to 63, 64 to 127, ..., all dimensions but the last counted through in order) at most 6 rows name the same one
- forward_gates: float32 [4, 2048, 6], P('phase', 'expert'), may hold values from 0.05 to 1
- hidden_rows: bfloat16 [4, 96, 32, 6, 1024], P('phase', 'expert', None, None, 'tensor'), may hold values from -6 to 6
- down_weight: bfloat16 [4, 96, 1024, 2560], P('phase', 'expert', 'tensor'), may hold values from -0.1875 to 0.1875
- shared_hidden: bfloat16 [4, 2048, 1536], P('phase', 'expert', 'tensor'), may hold values from -6 to 6
- shared_weight: bfloat16 [4, 1536, 2560], P('phase', 'tensor', 'expert'), may hold values from -0.15625 to 0.15625
- backward_routes: int32 [4, 2048, 6], P('phase', 'expert'), may hold values from 0 to 95, all different within a row; in each aligned block of 64 rows (0 to 63, 64 to 127, ..., all dimensions but the last counted through in order) at most 6 rows name the same one
- backward_gates: float32 [4, 2048, 6], P('phase', 'expert'), may hold values from 0.05 to 1
- cotangent: bfloat16 [4, 2048, 2560], P('phase', 'expert', 'tensor'), may hold values from -6 to 6
Outputs:
- forward_next: bfloat16 [4, 2048, 2560], P('phase', 'expert', 'tensor')
- hidden_grad: bfloat16 [4, 96, 32, 6, 1024], P('phase', 'expert', None, None, 'tensor')
- shared_grad: bfloat16 [4, 2048, 1536], P('phase', 'expert', 'tensor')
Inputs may be any that keep to these rules, and one draw needn't show every extreme that they name: `forward_routes`: each token names 6 different experts. The tokens of one token group (the 64 rows of one device) name any one expert 6 times at most, and some group reaches that. `backward_routes`: as for forward_routes.
All inputs are finite; a program needn't handle non-finite values.
Results may differ from a plain program's by a relative error of at most 0.0049.
Values may be sent and summed in bfloat16 or wider, within the bound.
No kernel may reach another device: no remote copies, remote signals or barrier semaphores. Data moves between devices by JAX's collectives and lax.ppermute only.
A program may use at most 64 MiB of HBM per device.

v0:
```python
import jax
import jax.numpy as jnp
from jax import lax
from jax.sharding import PartitionSpec as P


def in_blocks(array, dim, length):
    before, after = (array.shape[:dim], array.shape[dim + 1 :])
    return jnp.moveaxis(array.reshape(*before, length, -1, *after), dim, 0)


def summed_on_arrival(array, axis, dim):
    parts = in_blocks(array, dim, lax.axis_size(axis))
    arrived = lax.all_to_all(parts, axis, split_axis=0, concat_axis=0, tiled=True)
    return arrived.sum(axis=0)


def shifted(value, axis, steps):
    count = lax.axis_size(axis)
    pairs = [(source, (source + steps) % count) for source in range(count)]
    return lax.ppermute(value, axis, pairs)


def sent_to_all(array, axis):
    length = lax.axis_size(axis)
    return lax.all_to_all(
        jnp.broadcast_to(array[None], (length, *array.shape)), axis, 0, 0, tiled=True
    )


def joined_along(parts, dim):
    parts = jnp.moveaxis(parts, 0, dim)
    dims = parts.shape
    return parts.reshape(*dims[:dim], dims[dim] * dims[dim + 1], *dims[dim + 2 :])


def gathered_copies(array, axis, dim):
    parts = sent_to_all(array, axis)
    return joined_along(parts, dim)


def slot_numbers(routes, experts):
    numbers = jnp.arange(experts, dtype=jnp.int32)
    onehot = (routes[:, :, None] == numbers[None, None, :]).astype(jnp.int32)
    per_token = jnp.sum(onehot, axis=1)
    before = jnp.cumsum(per_token, axis=0) - per_token
    return jnp.sum(onehot * before[:, None, :], axis=2)


def row_positions(routes, experts_here, groups, capacity):
    slot_index = slot_numbers(routes, experts_here * groups)
    holder = routes // experts_here
    within = routes - holder * experts_here
    return ((within * groups + holder) * capacity + slot_index).reshape(-1)


def place_rows(gates, values, positions, total_rows):
    scaled = (gates[:, :, None] * values[:, None, :].astype(jnp.float32)).astype(jnp.bfloat16)
    outgoing = jnp.zeros((total_rows, values.shape[1]), jnp.bfloat16)
    return outgoing.at[positions].set(scaled.reshape(-1, values.shape[1]))


def on_device(
    forward_routes,
    forward_gates,
    hidden_rows,
    down_weight,
    shared_hidden,
    shared_weight,
    backward_routes,
    backward_gates,
    cotangent,
):
    experts_here = down_weight.shape[1]
    features = down_weight.shape[3]
    capacity = hidden_rows.shape[3]
    groups = lax.axis_size("expert")
    token_count = forward_routes.shape[1]
    top_count = forward_routes.shape[2]
    hidden = hidden_rows[0]
    weight = down_weight[0]
    local_shared = shared_hidden[0]
    shared_piece = shared_weight[0]
    shared_part = jnp.dot(
        local_shared,
        lax.all_gather(shared_piece, "expert", axis=1, tiled=True),
        preferred_element_type=jnp.float32,
    )
    fore_positions = row_positions(forward_routes[0], experts_here, groups, capacity)
    fore_gates = forward_gates[0]
    partial_value = jnp.einsum(
        "egmh,ehd->egmd", hidden, weight, preferred_element_type=jnp.float32
    ).astype(jnp.bfloat16)
    arrived = lax.all_to_all(partial_value, "expert", split_axis=1, concat_axis=1, tiled=True)
    picked = arrived.reshape(-1, features)[fore_positions].reshape(token_count, top_count, features)
    summand = shared_part + jnp.sum(picked.astype(jnp.float32) * fore_gates[:, :, None], axis=1)
    summed = summed_on_arrival(summand, "tensor", 1)
    layer_out = summed.astype(jnp.bfloat16)
    handed = shifted(layer_out, "phase", 1)
    cotangent_whole = gathered_copies(cotangent[0], "tensor", 1)
    back_positions = row_positions(backward_routes[0], experts_here, groups, capacity)
    total_rows = experts_here * groups * capacity
    local_cot = cotangent[0]
    outgoing = place_rows(backward_gates[0], local_cot, back_positions, total_rows)
    received_part = lax.all_to_all(
        outgoing.reshape(experts_here, groups, capacity, local_cot.shape[1]),
        "expert",
        split_axis=1,
        concat_axis=1,
        tiled=True,
    )
    received = lax.all_gather(received_part, "tensor", axis=3, tiled=True)
    hidden_back = jnp.einsum(
        "egmd,ehd->egmh", received, weight, preferred_element_type=jnp.float32
    ).astype(jnp.bfloat16)
    shared_back = lax.dot_general(
        cotangent_whole,
        lax.all_gather(shared_piece, "expert", axis=1, tiled=True),
        (((1,), (1,)), ((), ())),
        preferred_element_type=jnp.float32,
    )
    return (handed[None], hidden_back[None], shared_back.astype(jnp.bfloat16)[None])


def solution(mesh):
    return jax.shard_map(
        on_device,
        mesh=mesh,
        in_specs=(
            P("phase", "expert", None),
            P("phase", "expert", None),
            P("phase", "expert", None, None, "tensor"),
            P("phase", "expert", "tensor", None),
            P("phase", "expert", "tensor"),
            P("phase", "tensor", "expert"),
            P("phase", "expert", None),
            P("phase", "expert", None),
            P("phase", "expert", "tensor"),
        ),
        out_specs=(
            P("phase", "expert", "tensor"),
            P("phase", "expert", None, None, "tensor"),
            P("phase", "expert", "tensor"),
        ),
        check_vma=False,
    )
```

profile of v0, /device:TPU:49, one launch (start us, length us, event | category | flops | bytes accessed | tf_op | source)
XLA Modules:
  0.0 391.0 jit_solution(6066048009045506084)
XLA Ops:
  7.2 0.7 copy.57
  7.9 0.8 copy.41
  8.9 0.3 select_reduce_fusion
  9.6 0.9 bitcast_convert_fusion
  11.0 2.4 scatter_custom_fusion
  13.7 1.0 copy.44
  14.7 17.6 %all-to-all-start.2 = ((bf16[3,32,6,640]{3,2,0,1:T(8,128)(2,1)}), bf16[3,32,6,640]{3,2,0,1:T(8,128)(2,1)S(1)}, u32[]{:S(2)}, u32[]{:S(2)}) async-start(bf16[3,32,6,640]{3,2,0,1:T(8,128)(2,1)} %copy.44), calls=%async_computation.2 | async-start | bytes 1966080 | tf_op jit(solution)/shard_map/all_to_all | solution.py:105
  32.4 3.0 convolution_convert_fusion
  35.4 3.5 copy.35
  39.0 44.8 %all-to-all-done.2 = bf16[3,32,6,640]{3,2,0,1:T(8,128)(2,1)S(1)} async-done(((bf16[3,32,6,640]{3,2,0,1:T(8,128)(2,1)}), bf16[3,32,6,640]{3,2,0,1:T(8,128)(2,1)S(1)}, u32[]{:S(2)}, u32[]{:S(2)}) %all-to-all-start.2) | async-done | bytes 737312 | tf_op jit(solution)/shard_map/all_to_all | solution.py:105
  83.7 6.6 %all-to-all-start = ((bf16[3,32,6,2560]{3,2,0,1:T(8,128)(2,1)}), bf16[3,32,6,2560]{3,2,0,1:T(8,128)(2,1)}, u32[]{:S(2)}, u32[]{:S(2)}) async-start(bf16[3,32,6,2560]{3,2,0,1:T(8,128)(2,1)} %copy.35), calls=%async_computation | async-start | bytes 7864320 | tf_op jit(solution)/shard_map/all_to_all | solution.py:94
  90.4 0.7 all-gather.6.cloned.1.call-update
  91.2 1.0 copy.45
  92.2 198.5 %all-to-all-done = bf16[3,32,6,2560]{3,2,0,1:T(8,128)(2,1)} async-done(((bf16[3,32,6,2560]{3,2,0,1:T(8,128)(2,1)}), bf16[3,32,6,2560]{3,2,0,1:T(8,128)(2,1)}, u32[]{:S(2)}, u32[]{:S(2)}) %all-to-all-start) | async-done | bytes 2949152 | tf_op jit(solution)/shard_map/all_to_all | solution.py:94
  290.7 0.7 broadcast_in_dim.26
  291.5 4.3 %all-to-all-start.3 = ((bf16[4,64,640]{2,1,0:T(8,128)(2,1)}), bf16[4,64,640]{2,1,0:T(8,128)(2,1)}, u32[]{:S(2)}, u32[]{:S(2)}) async-start(bf16[4,64,640]{2,1,0:T(8,128)(2,1)} %broadcast_in_dim.26), calls=%async_computation.3 | async-start | bytes 655360 | tf_op jit(solution)/shard_map/all_to_all | solution.py:26
  296.1 0.3 select_reduce_fusion.1
  296.9 4.4 %copy.36 = bf16[3,32,6,2560]{3,2,1,0:T(8,128)(2,1)} copy(bf16[3,32,6,2560]{3,2,0,1:T(8,128)(2,1)} %all-to-all-done) | data formatting | bytes 5898240 | tf_op jit(solution)/shard_map/all_to_all | solution.py:94
  301.3 4.1 %reshape.226 = bf16[576,2560]{1,0:T(8,128)(2,1)S(1)} reshape(bf16[3,32,6,2560]{3,2,1,0:T(8,128)(2,1)} %copy.36) | data formatting | bytes 5898240 | tf_op jit(solution)/shard_map/reshape | solution.py:95
  305.4 3.3 gather_fusion
  308.6 4.5 %reshape.230 = f32[64,6,2560]{2,1,0:T(8,128)} reshape(bf16[384,2560]{1,0:T(8,128)(2,1)} %gather_fusion) | data formatting | bytes 5898240 | tf_op jit(solution)/shard_map/convert_element_type | solution.py:96
  313.1 4.8 %multiply_reduce_fusion = f32[64,2560]{1,0:T(8,128)S(1)} fusion(f32[64,6,2560]{2,1,0:T(8,128)} %reshape.230, f32[64,6]{1,0:T(8,128)S(1)} %bitcast.56), kind=kLoop, calls=%fused_computation.2 | loop fusion | flops 1802240 | bytes 4589056 | tf_op jit(solution)/shard_map/reduce_sum | solution.py:96
  317.9 2.4 convolution_add_fusion
  320.4 0.9 copy.56
  321.3 3.5 all-to-all-start.1
  324.7 1.0 copy.52
  325.8 1.1 fusion.15
  326.8 28.5 %all-to-all-done.1 = f32[4,64,640]{2,1,0:T(8,128)S(1)} async-done(((f32[4,64,640]{2,1,0:T(8,128)}), f32[4,64,640]{2,1,0:T(8,128)S(1)}, u32[]{:S(2)}, u32[]{:S(2)}) %all-to-all-start.1) | async-done | bytes 655392 | tf_op jit(solution)/shard_map/all_to_all | solution.py:14
  355.4 3.2 collective-permute-start
  358.6 19.8 %all-gather.4.cloned.1.call-done = bf16[3,32,6,2560]{3,1,2,0:T(8,128)(2,1)} async-done(((bf16[3,32,6,640]{3,1,2,0:T(8,128)(2,1)}), bf16[3,32,6,2560]{3,1,2,0:T(8,128)(2,1)}) %all-gather.4.cloned.1.call-update) | async-done | bytes 2949136 | tf_op jit(solution)/shard_map/all_gather | solution.py:112
  378.4 5.1 %fusion.9 = bf16[1,3,32,6,256]{4,2,3,1,0:T(8,128)(2,1)} fusion(bf16[3,32,6,2560]{3,1,2,0:T(8,128)(2,1)} %all-gather.4.cloned.1.call-done, bf16[1,3,256,2560]{3,2,1,0:T(8,128)(2,1)} %param.12), kind=kOutput, calls=%fused_computation.12 | convolution fusion | flops 755122176 | bytes 7176192 | tf_op jit(solution)/shard_map/egmd,ehd->egmh/dot_general | solution.py:113
  383.6 0.6 copy.60
  (44 shorter events, 2.4 us)
Async XLA Ops:
  7.2 25.2 %copy-start = (bf16[1,3,32,6,256]{4,2,3,1,0:T(8,128)(2,1)S(1)}, bf16[1,3,32,6,256]{4,2,3,1,0:T(8,128)(2,1)}, u32[]{:S(2)}) copy-start(bf16[1,3,32,6,256]{4,2,3,1,0:T(8,128)(2,1)} %param.11) | copy-start | bytes 884740
  7.2 3.6 copy-start.5
  14.7 69.0 %all-to-all-start.2 = ((bf16[3,32,6,640]{3,2,0,1:T(8,128)(2,1)}), bf16[3,32,6,640]{3,2,0,1:T(8,128)(2,1)S(1)}, u32[]{:S(2)}, u32[]{:S(2)}) async-start(bf16[3,32,6,640]{3,2,0,1:T(8,128)(2,1)} %copy.44), calls=%async_computation.2 | async-start | bytes 1966080 | tf_op jit(solution)/shard_map/all_to_all | solution.py:105
  39.0 53.3 %copy-start.4 = (s32[1,64,6]{1,0,2:T(1,128)S(1)}, s32[1,64,6]{1,0,2:T(1,128)}, u32[]{:S(2)}) copy-start(s32[1,64,6]{1,0,2:T(1,128)} %param.9) | copy-start | bytes 4612
  39.0 251.8 %copy-start.2 = (bf16[1,64,640]{2,1,0:T(8,128)(2,1)S(1)}, bf16[1,64,640]{2,1,0:T(8,128)(2,1)}, u32[]{:S(2)}) copy-start(bf16[1,64,640]{2,1,0:T(8,128)(2,1)} %param.17) | copy-start | bytes 245764
  83.7 207.0 %all-to-all-start = ((bf16[3,32,6,2560]{3,2,0,1:T(8,128)(2,1)}), bf16[3,32,6,2560]{3,2,0,1:T(8,128)(2,1)}, u32[]{:S(2)}, u32[]{:S(2)}) async-start(bf16[3,32,6,2560]{3,2,0,1:T(8,128)(2,1)} %copy.35), calls=%async_computation | async-start | bytes 7864320 | tf_op jit(solution)/shard_map/all_to_all | solution.py:94
  90.4 206.3 %copy-start.6 = (f32[1,64,6]{1,0,2:T(1,128)S(1)}, f32[1,64,6]{1,0,2:T(1,128)}, u32[]{:S(2)}) copy-start(f32[1,64,6]{1,0,2:T(1,128)} %param.10) | copy-start | bytes 4612
  90.4 227.5 %all-gather.6.cloned.1.call-start = ((), (), s32[]{:S(2)}) async-start(), calls=%async_computation.5 | async-start | bytes 2027520 | tf_op jit(solution)/shard_map/all_gather | solution.py:86
  91.1 287.3 %all-gather.4.cloned.1.call-start = ((), (), s32[]{:S(2)}) async-start(), calls=%async_computation.4 | async-start | bytes 3686400 | tf_op jit(solution)/shard_map/all_gather | solution.py:112
  291.5 29.8 %all-to-all-start.3 = ((bf16[4,64,640]{2,1,0:T(8,128)(2,1)}), bf16[4,64,640]{2,1,0:T(8,128)(2,1)}, u32[]{:S(2)}, u32[]{:S(2)}) async-start(bf16[4,64,640]{2,1,0:T(8,128)(2,1)} %broadcast_in_dim.26), calls=%async_computation.3 | async-start | bytes 655360 | tf_op jit(solution)/shard_map/all_to_all | solution.py:26
  313.1 4.8 %copy-start.3 = (bf16[1,64,384]{2,1,0:T(8,128)(2,1)S(1)}, bf16[1,64,384]{2,1,0:T(8,128)(2,1)}, u32[]{:S(2)}) copy-start(bf16[1,64,384]{2,1,0:T(8,128)(2,1)} %param.13) | copy-start | bytes 147460
  317.9 7.8 %copy-start.1 = (bf16[1,384,2560]{1,2,0:T(8,128)(2,1)S(1)}, bf16[1,384,2560]{1,2,0:T(8,128)(2,1)}, u32[]{:S(2)}) copy-start(bf16[1,384,2560]{1,2,0:T(8,128)(2,1)} %all-gather.6.cloned.1.call-done) | copy-start | bytes 5898244
  321.3 34.1 %all-to-all-start.1 = ((f32[4,64,640]{2,1,0:T(8,128)}), f32[4,64,640]{2,1,0:T(8,128)S(1)}, u32[]{:S(2)}, u32[]{:S(2)}) async-start(f32[4,64,640]{2,1,0:T(8,128)} %bitcast.50), calls=%async_computation.1 | async-start | bytes 1310720 | tf_op jit(solution)/shard_map/all_to_all | solution.py:14
  355.4 28.2 %collective-permute-start = (bf16[64,640]{1,0:T(8,128)(2,1)S(1)}, bf16[64,640]{1,0:T(8,128)(2,1)S(1)}, u32[]{:S(2)}, u32[]{:S(2)}) collective-permute-start(bf16[64,640]{1,0:T(8,128)(2,1)S(1)} %reduce_sum.62), channel_id=1, source_target_pairs={{0,128},{128,256},{256,384},{384,0},{1,129},{129,257},{257,385},{3... | collective-permute-start | bytes 245768 | tf_op jit(solution)/shard_map/ppermute | solution.py:21
Sparse Core Ops, SparseCore 0:
  94.4 201.1 all-gather.5
  297.8 80.5 all-gather.3
where the time goes:
time: 392 us; the launch traced here: 391 us
  waiting for transfers between devices  292 us (74%)
  starting transfers between devices  35.3 us (9%)
  local copies, waits for them, and re-layouts  28.3 us (7%)
  between operations  14.3 us (4%)
  matrix products  11.7 us (3%)
  other arithmetic  9.14 us (2%)
    all_to_all x1, waiting for transfers between devices, on_device(): lax.all_to_all(partial_value, 'expert', split_axis=1, concat_axis=1, tile...  198 us
    all_to_all x1, waiting for transfers between devices, on_device(): lax.all_to_all(outgoing.reshape(experts_here, groups, capacity, local_cot...  44.8 us
    all_to_all x1, waiting for transfers between devices, summed_on_arrival(): lax.all_to_all(parts, axis, split_axis=0, concat_axis=0, tiled=True)  28.5 us
    all_gather x1, waiting for transfers between devices, on_device(): received = lax.all_gather(received_part, 'tensor', axis=3, tiled=True)  19.8 us
    all_to_all x1, starting transfers between devices, on_device(): lax.all_to_all(outgoing.reshape(experts_here, groups, capacity, local_cot...  17.6 us
  transfers between devices with their start and end apart: 7, of which 4 were waited for; matrix products, arithmetic and copies ran while one was open for 10% of the time, Pallas kernels for 0%

commit v1 on v0

--- a/solution.py
+++ b/solution.py
@@ -2,6 +2,11 @@
 import jax.numpy as jnp
 from jax import lax
 from jax.sharding import PartitionSpec as P
+
+
+def exchange_gather(x, mesh_axis, dim):
+    stack = jnp.stack([x] * lax.axis_size(mesh_axis))
+    return jnp.concatenate(lax.all_to_all(stack, mesh_axis, 0, 0), axis=dim)
 
 
 def in_blocks(array, dim, length):
@@ -109,7 +114,7 @@
         concat_axis=1,
         tiled=True,
     )
-    received = lax.all_gather(received_part, "tensor", axis=3, tiled=True)
+    received = exchange_gather(received_part, "tensor", 3)
     hidden_back = jnp.einsum(
         "egmd,ehd->egmh", received, weight, preferred_element_type=jnp.float32
     ).astype(jnp.bfloat16)

time: 392 us -> 446 us (1.14)
  the two profiles are of different devices: /device:TPU:49 before, /device:TPU:1 now
where the time goes in v1:
time: 446 us; the launch traced here: 444 us
  waiting for transfers between devices  328 us (74%)
  starting transfers between devices  49.4 us (11%)
  local copies, waits for them, and re-layouts  32.5 us (7%)
  between operations  14.3 us (3%)
  matrix products  10.8 us (2%)
  other arithmetic  9.87 us (2%)
    all_to_all x1, waiting for transfers between devices, on_device(): lax.all_to_all(partial_value, 'expert', split_axis=1, concat_axis=1, tile...  174 us
    all_gather x1, waiting for transfers between devices, on_device(): lax.all_gather(shared_piece, 'expert', axis=1, tiled=True)  97.4 us
    all_to_all x1, waiting for transfers between devices, on_device(): lax.all_to_all(outgoing.reshape(experts_here, groups, capacity, local_cot...  42.8 us
    all_to_all x1, starting transfers between devices, on_device(): lax.all_to_all(outgoing.reshape(experts_here, groups, capacity, local_cot...  20.2 us
    all_to_all x1, waiting for transfers between devices, summed_on_arrival(): lax.all_to_all(parts, axis, split_axis=0, concat_axis=0, tiled=True)  12.9 us
  transfers between devices with their start and end apart: 7, of which 4 were waited for; matrix products, arithmetic and copies ran while one was open for 11% of the time, Pallas kernels for 0%

profile of v1, /device:TPU:1, one launch (start us, length us, event | category | flops | bytes accessed | tf_op | source)
XLA Modules:
  0.0 444.5 jit_solution(11174500284585571571)
XLA Ops:
  7.2 1.7 broadcast_in_dim.26
  8.9 6.4 %all-to-all-start.4 = ((bf16[4,64,640]{2,1,0:T(8,128)(2,1)}), bf16[4,64,640]{2,1,0:T(8,128)(2,1)}, u32[]{:S(2)}, u32[]{:S(2)}) async-start(bf16[4,64,640]{2,1,0:T(8,128)(2,1)} %broadcast_in_dim.26), calls=%async_computation.4 | async-start | bytes 655360 | tf_op jit(solution)/shard_map/all_to_all | solution.py:31
  15.3 0.7 copy.60
  16.0 0.8 copy.42
  17.7 0.9 bitcast_convert_fusion
  19.1 2.4 scatter_custom_fusion
  21.8 1.0 copy.45
  22.8 20.2 %all-to-all-start.2 = ((bf16[3,32,6,640]{3,2,0,1:T(8,128)(2,1)}), bf16[3,32,6,640]{3,2,0,1:T(8,128)(2,1)S(1)}, u32[]{:S(2)}, u32[]{:S(2)}) async-start(bf16[3,32,6,640]{3,2,0,1:T(8,128)(2,1)} %copy.45), calls=%async_computation.2 | async-start | bytes 1966080 | tf_op jit(solution)/shard_map/all_to_all | solution.py:110
  43.1 3.1 convolution_convert_fusion
  46.1 3.5 copy.36
  49.7 42.8 %all-to-all-done.2 = bf16[3,32,6,640]{3,2,0,1:T(8,128)(2,1)S(1)} async-done(((bf16[3,32,6,640]{3,2,0,1:T(8,128)(2,1)}), bf16[3,32,6,640]{3,2,0,1:T(8,128)(2,1)S(1)}, u32[]{:S(2)}, u32[]{:S(2)}) %all-to-all-start.2) | async-done | bytes 737312 | tf_op jit(solution)/shard_map/all_to_all | solution.py:110
  92.4 8.8 %all-to-all-start = ((bf16[3,32,6,2560]{3,2,0,1:T(8,128)(2,1)}), bf16[3,32,6,2560]{3,2,0,1:T(8,128)(2,1)}, u32[]{:S(2)}, u32[]{:S(2)}) async-start(bf16[3,32,6,2560]{3,2,0,1:T(8,128)(2,1)} %copy.36), calls=%async_computation | async-start | bytes 7864320 | tf_op jit(solution)/shard_map/all_to_all | solution.py:99
  101.4 173.9 %all-to-all-done = bf16[3,32,6,2560]{3,2,0,1:T(8,128)(2,1)} async-done(((bf16[3,32,6,2560]{3,2,0,1:T(8,128)(2,1)}), bf16[3,32,6,2560]{3,2,0,1:T(8,128)(2,1)}, u32[]{:S(2)}, u32[]{:S(2)}) %all-to-all-start) | async-done | bytes 2949152 | tf_op jit(solution)/shard_map/all_to_all | solution.py:99
  275.2 2.0 stack.2
  277.3 6.1 %all-to-all-start.3 = ((bf16[4,3,32,6,640]{4,2,3,1,0:T(8,128)(2,1)}), bf16[4,3,32,6,640]{4,2,3,1,0:T(8,128)(2,1)}, u32[]{:S(2)}, u32[]{:S(2)}) async-start(bf16[4,3,32,6,640]{4,2,3,1,0:T(8,128)(2,1)} %stack.2), calls=%async_computation.3 | async-start | bytes 5898240 | tf_op jit(solution)/shard_map/all_to_all | solution.py:9
  283.3 0.7 all-gather.3.cloned.1.call-update
  285.2 4.4 copy.37
  289.6 4.1 reshape.234
  293.7 3.3 gather_fusion
  297.0 4.5 %reshape.240 = f32[64,6,2560]{2,1,0:T(8,128)} reshape(bf16[384,2560]{1,0:T(8,128)(2,1)} %gather_fusion) | data formatting | bytes 5898240 | tf_op jit(solution)/shard_map/convert_element_type | solution.py:101
  301.5 4.4 multiply_reduce_fusion
  305.9 97.4 %all-gather.3.cloned.1.call-done = bf16[1,384,2560]{1,2,0:T(8,128)(2,1)} async-done(((bf16[1,384,80]{1,2,0:T(8,128)(2,1)}), bf16[1,384,2560]{1,2,0:T(8,128)(2,1)}) %all-gather.3.cloned.1.call-update) | async-done | bytes 1966096 | tf_op jit(solution)/shard_map/all_gather | solution.py:91
  403.3 2.4 convolution_add_fusion
  405.7 0.9 copy.59
  406.6 4.2 all-to-all-start.1
  410.8 1.0 copy.55
  411.8 1.1 fusion.15
  412.9 2.2 copy.54
  415.1 12.9 %all-to-all-done.1 = f32[4,64,640]{2,1,0:T(8,128)} async-done(((f32[4,64,640]{2,1,0:T(8,128)}), f32[4,64,640]{2,1,0:T(8,128)}, u32[]{:S(2)}, u32[]{:S(2)}) %all-to-all-start.1) | async-done | bytes 655392 | tf_op jit(solution)/shard_map/all_to_all | solution.py:19
  428.0 1.1 reduce_sum.62
  429.1 3.6 collective-permute-start
  432.8 4.2 fusion.9
  (43 shorter events, 3.5 us)
Async XLA Ops:
  7.2 35.9 %copy-start = (bf16[1,3,32,6,256]{4,2,3,1,0:T(8,128)(2,1)S(1)}, bf16[1,3,32,6,256]{4,2,3,1,0:T(8,128)(2,1)}, u32[]{:S(2)}) copy-start(bf16[1,3,32,6,256]{4,2,3,1,0:T(8,128)(2,1)} %param.11) | copy-start | bytes 884740
  7.2 11.6 %copy-start.4 = (f32[1,64,6]{1,0,2:T(1,128)S(1)}, f32[1,64,6]{1,0,2:T(1,128)}, u32[]{:S(2)}) copy-start(f32[1,64,6]{1,0,2:T(1,128)} %param.16) | copy-start | bytes 4612
  8.9 13.9 %all-to-all-start.4 = ((bf16[4,64,640]{2,1,0:T(8,128)(2,1)}), bf16[4,64,640]{2,1,0:T(8,128)(2,1)}, u32[]{:S(2)}, u32[]{:S(2)}) async-start(bf16[4,64,640]{2,1,0:T(8,128)(2,1)} %broadcast_in_dim.26), calls=%async_computation.4 | async-start | bytes 655360 | tf_op jit(solution)/shard_map/all_to_all | solution.py:31
  22.8 69.6 %all-to-all-start.2 = ((bf16[3,32,6,640]{3,2,0,1:T(8,128)(2,1)}), bf16[3,32,6,640]{3,2,0,1:T(8,128)(2,1)S(1)}, u32[]{:S(2)}, u32[]{:S(2)}) async-start(bf16[3,32,6,640]{3,2,0,1:T(8,128)(2,1)} %copy.45), calls=%async_computation.2 | async-start | bytes 1966080 | tf_op jit(solution)/shard_map/all_to_all | solution.py:110
  92.4 182.8 %all-to-all-start = ((bf16[3,32,6,2560]{3,2,0,1:T(8,128)(2,1)}), bf16[3,32,6,2560]{3,2,0,1:T(8,128)(2,1)}, u32[]{:S(2)}, u32[]{:S(2)}) async-start(bf16[3,32,6,2560]{3,2,0,1:T(8,128)(2,1)} %copy.36), calls=%async_computation | async-start | bytes 7864320 | tf_op jit(solution)/shard_map/all_to_all | solution.py:99
  277.2 6.8 %copy-start.3 = (s32[1,64,6]{1,0,2:T(1,128)S(1)}, s32[1,64,6]{1,0,2:T(1,128)}, u32[]{:S(2)}) copy-start(s32[1,64,6]{1,0,2:T(1,128)} %param.9) | copy-start | bytes 4612
  277.2 7.8 %copy-start.5 = (f32[1,64,6]{1,0,2:T(1,128)S(1)}, f32[1,64,6]{1,0,2:T(1,128)}, u32[]{:S(2)}) copy-start(f32[1,64,6]{1,0,2:T(1,128)} %param.10) | copy-start | bytes 4612
  277.3 129.3 %all-to-all-start.3 = ((bf16[4,3,32,6,640]{4,2,3,1,0:T(8,128)(2,1)}), bf16[4,3,32,6,640]{4,2,3,1,0:T(8,128)(2,1)}, u32[]{:S(2)}, u32[]{:S(2)}) async-start(bf16[4,3,32,6,640]{4,2,3,1,0:T(8,128)(2,1)} %stack.2), calls=%async_computation.3 | async-start | bytes 5898240 | tf_op jit(solution)/shard_map/all_to_all | solution.py:9
  283.3 119.9 %all-gather.3.cloned.1.call-start = ((), (), s32[]{:S(2)}) async-start(), calls=%async_computation.5 | async-start | bytes 2027520 | tf_op jit(solution)/shard_map/all_gather | solution.py:91
  301.5 101.8 %copy-start.2 = (bf16[1,64,384]{2,1,0:T(8,128)(2,1)S(1)}, bf16[1,64,384]{2,1,0:T(8,128)(2,1)}, u32[]{:S(2)}) copy-start(bf16[1,64,384]{2,1,0:T(8,128)(2,1)} %param.13) | copy-start | bytes 147460
  403.3 8.5 %copy-start.1 = (bf16[1,384,2560]{1,2,0:T(8,128)(2,1)S(1)}, bf16[1,384,2560]{1,2,0:T(8,128)(2,1)}, u32[]{:S(2)}) copy-start(bf16[1,384,2560]{1,2,0:T(8,128)(2,1)} %all-gather.3.cloned.1.call-done) | copy-start | bytes 5898244
  406.6 21.4 %all-to-all-start.1 = ((f32[4,64,640]{2,1,0:T(8,128)}), f32[4,64,640]{2,1,0:T(8,128)}, u32[]{:S(2)}, u32[]{:S(2)}) async-start(f32[4,64,640]{2,1,0:T(8,128)} %bitcast.53), calls=%async_computation.1 | async-start | bytes 1310720 | tf_op jit(solution)/shard_map/all_to_all | solution.py:19
  429.1 7.9 %collective-permute-start = (bf16[64,640]{1,0:T(8,128)(2,1)S(1)}, bf16[64,640]{1,0:T(8,128)(2,1)S(1)}, u32[]{:S(2)}, u32[]{:S(2)}) collective-permute-start(bf16[64,640]{1,0:T(8,128)(2,1)S(1)} %reduce_sum.62), channel_id=1, source_target_pairs={{0,128},{128,256},{256,384},{384,0},{1,129},{129,257},{257,385},{3... | collective-permute-start | bytes 245768 | tf_op jit(solution)/shard_map/ppermute | solution.py:26
Sparse Core Ops, SparseCore 0:
  287.4 115.8 all-gather.2
